TPU v7x, 256 devices: a whole 4x4x8 slice. The times are simulated.
256 devices in a mesh: seq: 16 (over x_lo, y, core), head: 8 (over z), batch: 2 (over x_hi).
Axes of the slice: x: 4 (x_hi: 2, x_lo: 2; x = x_hi * 2 + x_lo), y: 4, z: 8, core: 2. Of those that a mesh axis runs over, the one named last changes fastest.
Arguments:
- query_vectors: bfloat16 [4, 16384, 2048], P('batch', 'seq', 'head'), parts along dimension 0, may hold values from -6 to 6
- key_vectors: bfloat16 [4, 16384, 2048], P('batch', 'seq', 'head'), parts along dimension 0, may hold values from -6 to 6
- value_vectors: bfloat16 [4, 16384, 2048], P('batch', 'seq', 'head'), parts along dimension 0, may hold values from -6 to 6
- token_rates: float32 [4, 16, 16384], P('batch', 'head', 'seq'), parts along dimension 0, may hold values from 0.05 to 1
- gate_weight: float32 [16, 128, 256], P('head'), may hold values from -0.5 to 0.5
- up_weight: float32 [16, 128, 256], P('head'), may hold values from -0.5 to 0.5
- down_weight: float32 [16, 128, 256], P('head'), may hold values from -0.375 to 0.375
- step_sizes: float32 [16], P('head'), may hold values from 0.3 to 1
- norm_gain: float32 [2048], P('head'), may hold values from 0.1 to 1.9
Outputs:
- mixed: bfloat16 [4, 16384, 2048], P('batch', 'seq', 'head'), parts along dimension 0
- final_weights: float32 [6, 16, 128, 256], P('batch', 'head'), parts along dimension 0
There are 2 independent parts, one for each index of `batch`. A program takes and returns all parts, laid end to end along the dimension named above; an argument that names none is the same for every part. Nothing has to cross between parts.
All inputs are finite; a program needn't handle non-finite values.
Results may differ from a plain program's by a relative error of at most 0.008.
Values may be sent and summed in bfloat16 or wider, within the bound.
No kernel may reach another device: no remote copies, remote signals or barrier semaphores. Data moves between devices by JAX's collectives and lax.ppermute only.
A program may use at most 128 MiB of HBM per device.

v0:
```python
import functools
import math

import jax
import jax.numpy as jnp
from jax import lax
from jax.experimental import pallas as pl
from jax.experimental.pallas import tpu as pltpu
from jax.sharding import PartitionSpec as P

HD = 128
FW = 256
NS_STEPS = 5
ROWS = 256

coeff_first = 3.4445
coeff_second = -4.775
coeff_third = 2.0315
frob_epsilon = 1e-07
rms_epsilon = 1e-06
column_epsilon = 1e-06

f32 = jnp.float32
bf16 = jnp.bfloat16
LEAST_SUM = 1e-25
MOST_SUM = 1e30
VMEM_LIMIT = 48 * 1024 * 1024


def dot(a, b, over=((1,), (0,))):
    return lax.dot_general(a, b, (over, ((), ())), preferred_element_type=f32)


def sigmoid(x):
    return 0.5 * jnp.tanh(0.5 * x) + 0.5


def move(block, route):
    return lax.ppermute(block, "seq", [(i, route(i)) for i in range(lax.axis_size("seq"))])


def grads_kernel(k_ref, v_ref, r_ref, wg_ref, wu_ref, wd_ref, out_ref, grad_ref, hid_ref, og_ref):
    tokens = k_ref.shape[0]
    heads = r_ref.shape[0]
    for h in range(heads):
        lanes = slice(h * HD, (h + 1) * HD)
        low_gate = wg_ref[h].astype(bf16)
        low_up = wu_ref[h].astype(bf16)
        low_down = wd_ref[h].astype(bf16)
        for c in range(tokens // ROWS):
            rows = slice(c * ROWS, (c + 1) * ROWS)
            keys = k_ref[rows, lanes]
            rate = jnp.broadcast_to(r_ref[h : h + 1, rows], (HD, ROWS)).T
            out_grad = (-rate * v_ref[rows, lanes].astype(f32)).astype(bf16)
            gate_pre = dot(keys, low_gate)
            up_pre = dot(keys, low_up)
            hidden_grad = dot(out_grad, low_down)
            sig = sigmoid(gate_pre)
            active = gate_pre * sig
            og_ref[rows] = out_grad
            hid_ref[rows] = (active * up_pre).astype(bf16)
            grad_ref[rows, FW:] = (hidden_grad * active).astype(bf16)
            grad_ref[rows, :FW] = (
                hidden_grad * up_pre * sig * (1.0 + gate_pre * (1.0 - sig))
            ).astype(bf16)
        both = dot(k_ref[:, lanes], grad_ref[...], ((0,), (0,)))
        down = dot(og_ref[...], hid_ref[...], ((0,), (0,)))
        for which, full in enumerate((both[:, :FW], both[:, FW:], down)):
            for half in range(2):
                out_ref[(which * heads + h) * 2 + half] = full[
                    :, half * HD : (half + 1) * HD
                ].astype(out_ref.dtype)


def local_grads(keys, values, rates, weights):
    tokens, width = keys.shape
    heads = width // HD
    vmem = pl.BlockSpec(memory_space=pltpu.VMEM)
    return pl.pallas_call(
        grads_kernel,
        out_shape=jax.ShapeDtypeStruct((6 * heads, HD, HD), bf16),
        in_specs=[vmem] * 6,
        out_specs=vmem,
        scratch_shapes=[
            pltpu.VMEM((tokens, 2 * FW), bf16),
            pltpu.VMEM((tokens, FW), bf16),
            pltpu.VMEM((tokens, HD), bf16),
        ],
        compiler_params=pltpu.CompilerParams(vmem_limit_bytes=VMEM_LIMIT),
        cost_estimate=pl.CostEstimate(
            flops=12 * heads * tokens * HD * FW,
            bytes_accessed=4 * tokens * width,
            transcendentals=heads * tokens * FW,
        ),
        name="local_grads",
    )(keys, values, rates, *weights)


def split(x):
    high = x.astype(bf16)
    return high, (x - high.astype(f32)).astype(bf16)


def step_kernel(step_ref, s_ref, *refs):
    w_refs, first_refs, out_refs, x_ref = refs[:3], refs[3:6], refs[6:9], refs[9]
    heads = w_refs[0].shape[0]
    count = 3 * heads
    for m in range(count):
        grad = jnp.concatenate([s_ref[2 * m], s_ref[2 * m + 1]], axis=1).astype(f32)
        frobenius = jnp.sqrt(jnp.sum(grad * grad, keepdims=True))
        x_ref[m] = grad / (frobenius + frob_epsilon)

    def sweep(_, carry):
        pieces, polynomials = [], []
        for m in range(count):
            high, low = split(x_ref[m])
            pieces.append((high, low))
            stacked = jnp.concatenate([high, low], axis=0)
            g = dot(stacked, stacked, ((1,), (1,)))
            gram = g[:HD, :HD] + (g[HD:, :HD] + g[:HD, HD:]) + g[HD:, HD:]
            g_high, g_low = split(gram)
            row = jnp.concatenate([g_high, g_low], axis=1)
            squared = dot(row, jnp.concatenate([row, row], axis=0))
            polynomials.append(
                coeff_second * gram + coeff_third * (squared[:, :HD] + squared[:, HD:])
            )
        for m in range(count):
            high, low = pieces[m]
            row = jnp.concatenate(split(polynomials[m]), axis=1)
            product = dot(row, jnp.concatenate([high, high], axis=0)) + dot(
                row, jnp.concatenate([low, low], axis=0)
            )
            x_ref[m] = coeff_first * x_ref[m] + product
        return carry

    lax.fori_loop(0, NS_STEPS, sweep, 0)
    for which in range(3):
        for h in range(heads):
            first = first_refs[which][h]
            target = jnp.sqrt(jnp.sum(first * first, axis=0, keepdims=True))
            stepped = w_refs[which][h] - step_ref[h] * x_ref[which * heads + h]
            length = jnp.sqrt(jnp.sum(stepped * stepped, axis=0, keepdims=True))
            out_refs[which][h] = stepped * (target / (length + column_epsilon))


def step(summed, weights, first, step_sizes):
    heads = weights[0].shape[0]
    vmem = pl.BlockSpec(memory_space=pltpu.VMEM)
    return pl.pallas_call(
        step_kernel,
        out_shape=[jax.ShapeDtypeStruct(w.shape, f32) for w in weights],
        in_specs=[pl.BlockSpec(memory_space=pltpu.SMEM)] + [vmem] * 7,
        out_specs=[vmem] * 3,
        scratch_shapes=[pltpu.VMEM((3 * heads, HD, FW), f32)],
        compiler_params=pltpu.CompilerParams(vmem_limit_bytes=VMEM_LIMIT),
        cost_estimate=pl.CostEstimate(
            flops=3 * heads * NS_STEPS * 40 * HD * HD * FW,
            bytes_accessed=3 * heads * 10 * HD * FW,
            transcendentals=0,
        ),
        name="weight_step",
    )(step_sizes, summed, *weights, *first)


def mix_kernel(
    first_group,
    rank_ref,
    q_ref,
    ko_ref,
    vo_ref,
    kn_ref,
    vn_ref,
    kf_ref,
    vf_ref,
    wg_ref,
    wu_ref,
    wd_ref,
    gain_ref,
    out_ref,
    wide_own,
    wide_near,
    wide_far,
    attended_ref,
):
    tokens = q_ref.shape[0]
    scale = 1.0 / math.sqrt(HD)
    power = scale * math.log2(math.e)
    blocks = tokens // ROWS
    ones = jnp.ones((ROWS, HD), bf16)
    near_valid = rank_ref[0] >= 1 if first_group else True
    far_valid = rank_ref[0] >= 2 if first_group else True
    for wide, v_ref, valid in (
        (wide_own, vo_ref, True),
        (wide_near, vn_ref, near_valid),
        (wide_far, vf_ref, far_valid),
    ):
        for c in range(blocks):
            rows = slice(c * ROWS, (c + 1) * ROWS)
            block = jnp.concatenate([v_ref[rows], ones], axis=1)
            if valid is not True:
                block = block * jnp.where(valid, 1.0, 0.0).astype(bf16)
            wide[rows] = block
    causal = lax.broadcasted_iota(jnp.int32, (ROWS, ROWS), 0) >= lax.broadcasted_iota(
        jnp.int32, (ROWS, ROWS), 1
    )

    def raised(q, keys):
        return jnp.exp2(dot(q, keys, ((1,), (1,))) * power).astype(bf16)

    wrong = jnp.zeros((ROWS, HD), f32)
    for b in range(blocks):
        rows = slice(b * ROWS, (b + 1) * ROWS)
        q = q_ref[rows]
        own = dot(q, ko_ref[rows], ((1,), (1,)))
        far = dot(q, kf_ref[rows], ((1,), (1,)))
        edge = jnp.exp2(jnp.where(causal, own, far) * power)
        total = dot(jnp.where(causal, edge, 0.0).astype(bf16), wide_own[rows])
        total += dot(jnp.where(causal, 0.0, edge).astype(bf16), wide_far[rows])
        total += dot(raised(q, kn_ref[...]), wide_near[...])
        if b > 0:
            total += dot(raised(q, ko_ref[: b * ROWS]), wide_own[: b * ROWS])
        if b < blocks - 1:
            total += dot(raised(q, kf_ref[(b + 1) * ROWS :]), wide_far[(b + 1) * ROWS :])
        sums = total[:, HD:]
        attended_ref[rows] = total[:, :HD] / sums
        fine = (sums > LEAST_SUM) & (sums < MOST_SUM)
        wrong = jnp.maximum(wrong, jnp.where(fine, 0.0, 1.0))

    @pl.when(jnp.max(wrong) > 0.0)
    def _():
        def one_block(b, carry):
            rows = pl.ds(pl.multiple_of(b * ROWS, ROWS), ROWS)
            q = q_ref[rows]
            place = b * ROWS + lax.broadcasted_iota(jnp.int32, (ROWS, tokens), 0)
            column = lax.broadcasted_iota(jnp.int32, (ROWS, tokens), 1)
            limit = jnp.where(far_valid, tokens, -1)
            least = jnp.where(near_valid, 0, tokens)
            lowest = jnp.float32(-jnp.inf)
            far = dot(q, kf_ref[...], ((1,), (1,))) * scale
            far = jnp.where((column > place) & (column < limit), far, lowest)
            near = dot(q, kn_ref[...], ((1,), (1,))) * scale
            near = jnp.where(column >= least, near, lowest)
            own = dot(q, ko_ref[...], ((1,), (1,))) * scale
            own = jnp.where(column <= place, own, lowest)
            most = jnp.maximum(
                jnp.maximum(
                    jnp.max(far, axis=1, keepdims=True), jnp.max(near, axis=1, keepdims=True)
                ),
                jnp.max(own, axis=1, keepdims=True),
            )
            total = jnp.zeros((ROWS, HD), f32)
            sums = jnp.zeros((ROWS, 1), f32)
            for scores, v_ref in ((far, vf_ref), (near, vn_ref), (own, vo_ref)):
                e = jnp.exp(scores - most)
                sums += jnp.sum(e, axis=1, keepdims=True)
                total += dot(e.astype(bf16), v_ref[...])
            attended_ref[rows] = total / sums
            return carry

        lax.fori_loop(0, blocks, one_block, 0)

    low_gate = wg_ref[0].astype(bf16)
    low_up = wu_ref[0].astype(bf16)
    low_down = wd_ref[0].astype(bf16)
    for b in range(blocks):
        rows = slice(b * ROWS, (b + 1) * ROWS)
        q = q_ref[rows]
        gate_pre = dot(q, low_gate)
        hidden = (gate_pre * sigmoid(gate_pre) * dot(q, low_up)).astype(bf16)
        applied = dot(hidden, low_down, ((1,), (1,)))
        mean = jnp.mean(applied * applied, axis=1, keepdims=True)
        normed = applied * lax.rsqrt(mean + rms_epsilon) * gain_ref[...]
        out_ref[rows] = (normed + attended_ref[rows]).astype(bf16)


def mix(first_group, rank, queries, own, near, far, weights, gain):
    tokens, width = queries.shape
    heads = width // HD
    head = pl.BlockSpec((tokens, HD), lambda h: (0, h))
    weight = pl.BlockSpec((1, HD, FW), lambda h: (h, 0, 0))
    return pl.pallas_call(
        functools.partial(mix_kernel, first_group),
        out_shape=jax.ShapeDtypeStruct((tokens, width), bf16),
        grid=(heads,),
        in_specs=[pl.BlockSpec(memory_space=pltpu.SMEM)]
        + [head] * 7
        + [weight] * 3
        + [pl.BlockSpec((1, HD), lambda h: (0, h))],
        out_specs=head,
        scratch_shapes=[pltpu.VMEM((tokens, 2 * HD), bf16)] * 3 + [pltpu.VMEM((tokens, HD), f32)],
        compiler_params=pltpu.CompilerParams(vmem_limit_bytes=VMEM_LIMIT),
        cost_estimate=pl.CostEstimate(
            flops=heads * tokens * 2 * tokens * 8 * HD,
            bytes_accessed=16 * tokens * width,
            transcendentals=heads * tokens * 2 * tokens,
        ),
        name="mix",
    )(rank, queries, *own, *near, *far, *weights, gain)


def sum_over_seq(partial):
    size = lax.axis_size("seq")
    tiles = partial.reshape(size, -1, HD)
    arrived = lax.all_to_all(tiles, "seq", 0, 0, tiled=True)
    part = jnp.sum(arrived.astype(f32), axis=0).astype(bf16)
    copies = jnp.broadcast_to(part, tiles.shape)
    return lax.all_to_all(copies, "seq", 0, 0, tiled=True).reshape(partial.shape)


def body(
    query_vectors,
    key_vectors,
    value_vectors,
    token_rates,
    gate_weight,
    up_weight,
    down_weight,
    step_sizes,
    norm_gain,
):
    rank = lax.axis_index("seq")
    size = lax.axis_size("seq")
    first = (gate_weight, up_weight, down_weight)
    gain = norm_gain.reshape(1, -1)
    ranks = rank.astype(jnp.int32).reshape(1)
    groups = query_vectors.shape[0]
    own = [(key_vectors[g], value_vectors[g]) for g in range(groups)]
    context = []
    for g in range(groups):
        sent = own[g]
        if g > 0:
            sent = tuple(jnp.where(rank >= size - 2, a, b) for a, b in zip(own[g - 1], own[g]))
        far = tuple(move(a, lambda i: (i + 2) % size) for a in sent)
        near = tuple(
            move(jnp.where(rank % 2 == 0, a, b), lambda i: i ^ 1) for a, b in zip(own[g], far)
        )
        context.append((near, far))
    weights = first
    mixed = []
    for g in range(groups):
        partial = local_grads(*own[g], token_rates[g], weights)
        summed = sum_over_seq(partial)
        mixed.append(mix(g == 0, ranks, query_vectors[g], own[g], *context[g], weights, gain))
        weights = step(summed, weights, first, step_sizes)
    return jnp.stack(mixed), jnp.stack(weights)


def solution(mesh):
    return jax.shard_map(
        body,
        mesh=mesh,
        in_specs=(
            P("batch", "seq", "head"),
            P("batch", "seq", "head"),
            P("batch", "seq", "head"),
            P("batch", "head", "seq"),
            P("head", None, None),
            P("head", None, None),
            P("head", None, None),
            P("head"),
            P("head"),
        ),
        out_specs=(P("batch", "seq", "head"), P("batch", "head", None, None)),
        check_vma=False,
    )
```

profile of v0, /device:TPU:1, one launch (start us, length us, event | category | flops | bytes accessed | tf_op | source)
XLA Modules:
  0.0 145.3 jit_solution(4918219750850348393)
XLA Ops:
  0.6 1.4 slice_bitcast_fusion.4
  2.1 2.2 %collective-permute-start = (bf16[1024,256]{1,0:T(8,128)(2,1)S(1)}, bf16[1024,256]{1,0:T(8,128)(2,1)S(1)}, u32[]{:S(2)}, u32[]{:S(2)}) collective-permute-start(bf16[1024,256]{1,0:T(8,128)(2,1)S(1)} %get-tuple-element.22.ko_ref.k_ref), channel_id=1, source_target_pairs={{0,32},{16,48},{32,64},{48,80},{64,96},{80,112},{96,128},{112,144}... | collective-permute-start | bytes 1572872 | tf_op jit(solution)/shard_map/ppermute | solution.py:39
  4.4 2.8 %local_grads.2 = bf16[12,128,128]{2,1,0:T(8,128)(2,1)} custom-call(bf16[1024,256]{1,0:T(8,128)(2,1)S(1)} %get-tuple-element.22.ko_ref.k_ref, bf16[1024,256]{1,0:T(8,128)(2,1)S(1)} %get-tuple-element.20.vo_ref.v_ref, f32[2,1024]{1,0:T(2,128)S(1)} %get-tuple-element.25.r_ref, f32[2,128,256]{2,1,0:T(8,128)S(1)} %copy-done.8, f32[2,128,256]{2,1,0:T(8,128)S(1)} %copy-done.12, ...), custom_call_target="tpu_custom_call" | custom-call | flops 805306368 | bytes 1048576 | tf_op jit(solution)/shard_map/local_grads/pallas_call | solution.py:79
  7.2 6.5 %all-to-all-start = ((bf16[16,96,128]{2,1,0:T(8,128)(2,1)}), bf16[16,96,128]{2,1,0:T(8,128)(2,1)S(1)}, u32[]{:S(2)}, u32[]{:S(2)}) async-start(bf16[16,96,128]{2,1,0:T(8,128)(2,1)} %bitcast.10), calls=%async_computation | async-start | bytes 786432 | tf_op jit(solution)/shard_map/all_to_all | solution.py:304
  13.8 1.5 %collective-permute-start.2 = (bf16[1024,256]{1,0:T(8,128)(2,1)S(1)}, bf16[1024,256]{1,0:T(8,128)(2,1)S(1)}, u32[]{:S(2)}, u32[]{:S(2)}) collective-permute-start(bf16[1024,256]{1,0:T(8,128)(2,1)S(1)} %get-tuple-element.20.vo_ref.v_ref), channel_id=1, source_target_pairs={{0,32},{16,48},{32,64},{48,80},{64,96},{80,112},{96,128},{112,144}... | collective-permute-start | bytes 1572872 | tf_op jit(solution)/shard_map/ppermute | solution.py:39
  15.2 2.2 %slice_bitcast_fusion.5 = (bf16[1024,256]{1,0:T(8,128)(2,1)}, bf16[1024,256]{1,0:T(8,128)(2,1)}) fusion(bf16[2,1024,256]{2,1,0:T(8,128)(2,1)} %param.9), kind=kLoop, calls=%fused_computation.7 | loop fusion | bytes 2097152 | tf_op jit(solution)/shard_map/squeeze | solution.py:343
  17.5 6.7 %all-to-all-done = bf16[16,96,128]{2,1,0:T(8,128)(2,1)S(1)} async-done(((bf16[16,96,128]{2,1,0:T(8,128)(2,1)}), bf16[16,96,128]{2,1,0:T(8,128)(2,1)S(1)}, u32[]{:S(2)}, u32[]{:S(2)}) %all-to-all-start) | async-done | bytes 393248 | tf_op jit(solution)/shard_map/all_to_all | solution.py:304
  24.9 1.5 %broadcast_in_dim.6 = bf16[16,96,128]{2,1,0:T(8,128)(2,1)} broadcast(bf16[96,128]{1,0:T(8,128)(2,1)} %reduce_sum.24), dimensions={1,2} | broadcast | bytes 417792 | tf_op jit(solution)/shard_map/broadcast_in_dim | solution.py:306
  26.4 3.9 %all-to-all-start.1 = ((bf16[16,96,128]{2,1,0:T(8,128)(2,1)}), bf16[16,96,128]{2,1,0:T(8,128)(2,1)S(1)}, u32[]{:S(2)}, u32[]{:S(2)}) async-start(bf16[16,96,128]{2,1,0:T(8,128)(2,1)} %broadcast_in_dim.6), calls=%async_computation.1 | async-start | bytes 786432 | tf_op jit(solution)/shard_map/all_to_all | solution.py:307
  30.3 2.3 %broadcast_select_fusion.5 = (bf16[1024,256]{1,0:T(8,128)(2,1)}, bf16[1024,256]{1,0:T(8,128)(2,1)}) fusion(bf16[1024,256]{1,0:T(8,128)(2,1)S(1)} %collective-permute-done.kf_ref, pred[]{:T(512)S(6)} %eq.11, bf16[2,1024,256]{2,1,0:T(8,128)(2,1)} %param.10, pred[]{:T(512)S(6)} %ge.4), kind=kLoop, calls=%fused_computation.13 | loop fusion | flops 524288 | bytes 2621442 | tf_op jit(solution)/shard_map/jit(_where)/select_n | solution.py:335
  32.7 1.7 %collective-permute-done.2.vf_ref = bf16[1024,256]{1,0:T(8,128)(2,1)S(1)} collective-permute-done((bf16[1024,256]{1,0:T(8,128)(2,1)S(1)}, bf16[1024,256]{1,0:T(8,128)(2,1)S(1)}, u32[]{:S(2)}, u32[]{:S(2)}) %collective-permute-start.2) | collective-permute-done | bytes 524320 | tf_op jit(solution)/shard_map/ppermute | solution.py:39
  34.4 1.1 broadcast_select_fusion.4
  35.5 0.8 collective-permute-start.3
  36.4 1.2 collective-permute-start.6
  37.5 1.1 all-to-all-done.1
  38.7 0.9 copy-done.9
  39.6 0.9 copy-done.13
  40.6 0.9 copy-done.17
  41.5 9.1 %weight_step.2 = (f32[2,128,256]{2,1,0:T(8,128)S(1)}, f32[2,128,256]{2,1,0:T(8,128)S(1)}, f32[2,128,256]{2,1,0:T(8,128)S(1)}) custom-call(f32[2]{0:T(128)S(1)} %copy-done.21, bf16[12,128,128]{2,1,0:T(8,128)(2,1)S(1)} %bitcast.45, f32[2,128,256]{2,1,0:T(8,128)S(1)} %copy-done.9, f32[2,128,256]{2,1,0:T(8,128)S(1)} %copy-done.13, ...), custom_call_target="tpu_custom_call" | custom-call | flops 5033164800 | bytes 1966080 | tf_op jit(solution)/shard_map/weight_step/pallas_call | solution.py:149
  50.6 2.7 %local_grads.3 = bf16[12,128,128]{2,1,0:T(8,128)(2,1)} custom-call(bf16[1024,256]{1,0:T(8,128)(2,1)S(1)} %get-tuple-element.23.ko_ref.k_ref, bf16[1024,256]{1,0:T(8,128)(2,1)S(1)} %get-tuple-element.21.vo_ref.v_ref, f32[2,1024]{1,0:T(2,128)S(1)} %get-tuple-element.24.r_ref, f32[2,128,256]{2,1,0:T(8,128)S(1)} %get-tuple-element.8.wg_ref.refs_0_, ...), custom_call_target="tpu_custom_call" | custom-call | flops 805306368 | bytes 1048576 | tf_op jit(solution)/shard_map/local_grads/pallas_call | solution.py:79
  53.4 4.7 %all-to-all-start.2 = ((bf16[16,96,128]{2,1,0:T(8,128)(2,1)}), bf16[16,96,128]{2,1,0:T(8,128)(2,1)S(1)}, u32[]{:S(2)}, u32[]{:S(2)}) async-start(bf16[16,96,128]{2,1,0:T(8,128)(2,1)} %bitcast.14), calls=%async_computation.2 | async-start | bytes 786432 | tf_op jit(solution)/shard_map/all_to_all | solution.py:304
  58.1 2.0 %broadcast_select_fusion.3 = bf16[1024,256]{1,0:T(8,128)(2,1)} fusion(bf16[1024,256]{1,0:T(8,128)(2,1)S(1)} %collective-permute-done.4.kf_ref, pred[]{:T(512)S(6)} %eq.11, bf16[2,1024,256]{2,1,0:T(8,128)(2,1)} %param.10), kind=kLoop, calls=%fused_computation.11 | loop fusion | flops 262144 | bytes 1572865 | tf_op jit(solution)/shard_map/jit(_where)/select_n | solution.py:335
  60.2 4.1 %collective-permute-done.6.vf_ref = bf16[1024,256]{1,0:T(8,128)(2,1)S(1)} collective-permute-done((bf16[1024,256]{1,0:T(8,128)(2,1)}, bf16[1024,256]{1,0:T(8,128)(2,1)S(1)}, u32[]{:S(2)}, u32[]{:S(2)}) %collective-permute-start.6) | collective-permute-done | bytes 524320 | tf_op jit(solution)/shard_map/ppermute | solution.py:39
  64.3 0.9 broadcast_select_fusion.2
  65.2 1.4 collective-permute-start.7
  66.6 1.1 all-to-all-done.2
  67.7 0.7 reduce_sum.25
  68.3 1.5 %broadcast_in_dim.7 = bf16[16,96,128]{2,1,0:T(8,128)(2,1)} broadcast(bf16[96,128]{1,0:T(8,128)(2,1)} %reduce_sum.25), dimensions={1,2} | broadcast | bytes 417792 | tf_op jit(solution)/shard_map/broadcast_in_dim | solution.py:306
  69.9 4.3 %all-to-all-start.3 = ((bf16[16,96,128]{2,1,0:T(8,128)(2,1)}), bf16[16,96,128]{2,1,0:T(8,128)(2,1)S(1)}, u32[]{:S(2)}, u32[]{:S(2)}) async-start(bf16[16,96,128]{2,1,0:T(8,128)(2,1)} %broadcast_in_dim.7), calls=%async_computation.3 | async-start | bytes 786432 | tf_op jit(solution)/shard_map/all_to_all | solution.py:307
  74.2 0.7 copy-done.20
  74.9 1.0 copy-done.1
  75.9 1.0 copy-done.3
  77.0 1.0 copy-done.5
  78.0 0.9 copy-done.10
  79.0 0.9 copy-done.14
  79.9 0.9 copy-done.18
  80.9 22.9 %mix.2 = bf16[1024,256]{1,0:T(8,128)(2,1)S(1)} custom-call(s32[1]{0:T(128)} %bitcast.rank_ref, bf16[1024,256]{1,0:T(8,128)(2,1)S(1)} %copy-done.5, bf16[1024,256]{1,0:T(8,128)(2,1)S(1)} %copy-done.1, bf16[1024,256]{1,0:T(8,128)(2,1)S(1)} %copy-done.3, bf16[1024,256]{1,0:T(8,128)(2,1)} %collective-permute-done.1.kn_ref, ...), custom_call_target="tpu_custom_call" | custom-call | flops 4294967296 | bytes 4194304 | tf_op jit(solution)/shard_map/mix/pallas_call | solution.py:281
  103.8 0.8 copy-done.6
  104.6 0.9 copy-done.11
  105.6 0.9 copy-done.15
  106.5 0.9 copy-done.19
  107.5 0.9 copy-done.23
  108.4 0.9 copy-done.26
  109.4 0.9 copy-done.29
  110.3 9.1 %weight_step.3 = (f32[2,128,256]{2,1,0:T(8,128)S(1)}, f32[2,128,256]{2,1,0:T(8,128)S(1)}, f32[2,128,256]{2,1,0:T(8,128)S(1)}) custom-call(f32[2]{0:T(128)S(1)} %copy-done.21, bf16[12,128,128]{2,1,0:T(8,128)(2,1)S(1)} %bitcast.46, f32[2,128,256]{2,1,0:T(8,128)S(1)} %copy-done.23, f32[2,128,256]{2,1,0:T(8,128)S(1)} %copy-done.26, ...), custom_call_target="tpu_custom_call" | custom-call | flops 5033164800 | bytes 1966080 | tf_op jit(solution)/shard_map/weight_step/pallas_call | solution.py:149
  119.5 1.0 pad_maximum_fusion.1
  121.0 23.3 %mix.3 = bf16[1024,256]{1,0:T(8,128)(2,1)S(1)} custom-call(s32[1]{0:T(128)} %bitcast.rank_ref, bf16[1024,256]{1,0:T(8,128)(2,1)S(1)} %copy-done.4, bf16[1024,256]{1,0:T(8,128)(2,1)S(1)} %get-tuple-element.23.ko_ref.k_ref, bf16[1024,256]{1,0:T(8,128)(2,1)S(1)} %get-tuple-element.21.vo_ref.v_ref, bf16[1024,256]{1,0:T(8,128)(2,1)} %collective-permute-done.5.kn_ref, ...), custom_call_target="tpu_custom_call" | custom-call | flops 4294967296 | bytes 4194304 | tf_op jit(solution)/shard_map/mix/pallas_call | solution.py:281
  144.3 1.1 pad_maximum_fusion
  (66 shorter events, 1.6 us)
Async XLA Ops:
  0.6 3.6 %copy-start.31 = (bf16[2,1024,256]{2,1,0:T(8,128)(2,1)S(1)}, bf16[2,1024,256]{2,1,0:T(8,128)(2,1)}, u32[]{:S(2)}) copy-start(bf16[2,1024,256]{2,1,0:T(8,128)(2,1)} %param.11) | copy-start | bytes 3145732
  2.0 2.4 %copy-start = (bf16[1024,256]{1,0:T(8,128)(2,1)}, bf16[1024,256]{1,0:T(8,128)(2,1)S(1)}, u32[]{:S(2)}) copy-start(bf16[1024,256]{1,0:T(8,128)(2,1)S(1)} %get-tuple-element.22.ko_ref.k_ref) | copy-start | bytes 1572868
  2.0 2.3 %copy-start.34 = (f32[2,2,1024]{2,1,0:T(2,128)S(1)}, f32[2,2,1024]{2,1,0:T(2,128)}, u32[]{:S(2)}) copy-start(f32[2,2,1024]{2,1,0:T(2,128)} %param.12) | copy-start | bytes 49156
  2.0 2.4 %copy-start.8 = (f32[2,128,256]{2,1,0:T(8,128)S(1)}, f32[2,128,256]{2,1,0:T(8,128)}, u32[]{:S(2)}) copy-start(f32[2,128,256]{2,1,0:T(8,128)} %refs_3_.3) | copy-start | bytes 786436
  2.0 2.4 %copy-start.12 = (f32[2,128,256]{2,1,0:T(8,128)S(1)}, f32[2,128,256]{2,1,0:T(8,128)}, u32[]{:S(2)}) copy-start(f32[2,128,256]{2,1,0:T(8,128)} %refs_4_.3) | copy-start | bytes 786436
  2.0 2.4 %copy-start.16 = (f32[2,128,256]{2,1,0:T(8,128)S(1)}, f32[2,128,256]{2,1,0:T(8,128)}, u32[]{:S(2)}) copy-start(f32[2,128,256]{2,1,0:T(8,128)} %refs_5_.3) | copy-start | bytes 786436
  2.1 28.2 %collective-permute-start = (bf16[1024,256]{1,0:T(8,128)(2,1)S(1)}, bf16[1024,256]{1,0:T(8,128)(2,1)S(1)}, u32[]{:S(2)}, u32[]{:S(2)}) collective-permute-start(bf16[1024,256]{1,0:T(8,128)(2,1)S(1)} %get-tuple-element.22.ko_ref.k_ref), channel_id=1, source_target_pairs={{0,32},{16,48},{32,64},{48,80},{64,96},{80,112},{96,128},{112,144}... | collective-permute-start | bytes 1572872 | tf_op jit(solution)/shard_map/ppermute | solution.py:39
  4.3 9.4 %copy-start.2 = (bf16[1024,256]{1,0:T(8,128)(2,1)}, bf16[1024,256]{1,0:T(8,128)(2,1)S(1)}, u32[]{:S(2)}) copy-start(bf16[1024,256]{1,0:T(8,128)(2,1)S(1)} %get-tuple-element.20.vo_ref.v_ref) | copy-start | bytes 1572868
  7.2 17.0 %all-to-all-start = ((bf16[16,96,128]{2,1,0:T(8,128)(2,1)}), bf16[16,96,128]{2,1,0:T(8,128)(2,1)S(1)}, u32[]{:S(2)}, u32[]{:S(2)}) async-start(bf16[16,96,128]{2,1,0:T(8,128)(2,1)} %bitcast.10), calls=%async_computation | async-start | bytes 786432 | tf_op jit(solution)/shard_map/all_to_all | solution.py:304
  13.8 20.7 %collective-permute-start.2 = (bf16[1024,256]{1,0:T(8,128)(2,1)S(1)}, bf16[1024,256]{1,0:T(8,128)(2,1)S(1)}, u32[]{:S(2)}, u32[]{:S(2)}) collective-permute-start(bf16[1024,256]{1,0:T(8,128)(2,1)S(1)} %get-tuple-element.20.vo_ref.v_ref), channel_id=1, source_target_pairs={{0,32},{16,48},{32,64},{48,80},{64,96},{80,112},{96,128},{112,144}... | collective-permute-start | bytes 1572872 | tf_op jit(solution)/shard_map/ppermute | solution.py:39
  26.4 12.3 %all-to-all-start.1 = ((bf16[16,96,128]{2,1,0:T(8,128)(2,1)}), bf16[16,96,128]{2,1,0:T(8,128)(2,1)S(1)}, u32[]{:S(2)}, u32[]{:S(2)}) async-start(bf16[16,96,128]{2,1,0:T(8,128)(2,1)} %broadcast_in_dim.6), calls=%async_computation.1 | async-start | bytes 786432 | tf_op jit(solution)/shard_map/all_to_all | solution.py:307
  30.3 4.2 %copy-start.32 = (bf16[2,1024,256]{2,1,0:T(8,128)(2,1)S(1)}, bf16[2,1024,256]{2,1,0:T(8,128)(2,1)}, u32[]{:S(2)}) copy-start(bf16[2,1024,256]{2,1,0:T(8,128)(2,1)} %param.11) | copy-start | bytes 3145732
  32.6 41.6 %collective-permute-start.1 = (bf16[1024,256]{1,0:T(8,128)(2,1)}, bf16[1024,256]{1,0:T(8,128)(2,1)}, u32[]{:S(2)}, u32[]{:S(2)}) collective-permute-start(bf16[1024,256]{1,0:T(8,128)(2,1)} %get-tuple-element.16), channel_id=1, source_target_pairs={{0,16},{16,0},{32,48},{48,32},{64,80},{80,64},{96,112},{112,96},{1... | collective-permute-start | bytes 1572872 | tf_op jit(solution)/shard_map/ppermute | solution.py:39
  35.5 38.7 %collective-permute-start.3 = (bf16[1024,256]{1,0:T(8,128)(2,1)}, bf16[1024,256]{1,0:T(8,128)(2,1)}, u32[]{:S(2)}, u32[]{:S(2)}) collective-permute-start(bf16[1024,256]{1,0:T(8,128)(2,1)} %get-tuple-element.14), channel_id=1, source_target_pairs={{0,16},{16,0},{32,48},{48,32},{64,80},{80,64},{96,112},{112,96},{1... | collective-permute-start | bytes 1572872 | tf_op jit(solution)/shard_map/ppermute | solution.py:39
  36.4 21.7 %collective-permute-start.4 = (bf16[1024,256]{1,0:T(8,128)(2,1)}, bf16[1024,256]{1,0:T(8,128)(2,1)S(1)}, u32[]{:S(2)}, u32[]{:S(2)}) collective-permute-start(bf16[1024,256]{1,0:T(8,128)(2,1)} %get-tuple-element.17), channel_id=1, source_target_pairs={{0,32},{16,48},{32,64},{48,80},{64,96},{80,112},{96,128},{112,144}... | collective-permute-start | bytes 1572872 | tf_op jit(solution)/shard_map/ppermute | solution.py:39
  36.4 2.3 %copy-start.21 = (f32[2]{0:T(128)S(1)}, f32[2]{0:T(128)}, u32[]{:S(2)}) copy-start(f32[2]{0:T(128)} %step_ref.3) | copy-start | bytes 28
  36.4 27.9 %collective-permute-start.6 = (bf16[1024,256]{1,0:T(8,128)(2,1)}, bf16[1024,256]{1,0:T(8,128)(2,1)S(1)}, u32[]{:S(2)}, u32[]{:S(2)}) collective-permute-start(bf16[1024,256]{1,0:T(8,128)(2,1)} %get-tuple-element.15), channel_id=1, source_target_pairs={{0,32},{16,48},{32,64},{48,80},{64,96},{80,112},{96,128},{112,144}... | collective-permute-start | bytes 1572872 | tf_op jit(solution)/shard_map/ppermute | solution.py:39
  38.7 1.0 copy-start.9
  39.6 0.9 copy-start.13
  40.6 0.9 copy-start.17
  50.6 2.8 %copy-start.22 = (f32[2,128,256]{2,1,0:T(8,128)}, f32[2,128,256]{2,1,0:T(8,128)S(1)}, u32[]{:S(2)}) copy-start(f32[2,128,256]{2,1,0:T(8,128)S(1)} %get-tuple-element.8.wg_ref.refs_0_) | copy-start | bytes 786436
  50.6 2.8 %copy-start.25 = (f32[2,128,256]{2,1,0:T(8,128)}, f32[2,128,256]{2,1,0:T(8,128)S(1)}, u32[]{:S(2)}) copy-start(f32[2,128,256]{2,1,0:T(8,128)S(1)} %get-tuple-element.9.wu_ref.refs_1_) | copy-start | bytes 786436
  50.6 2.7 %copy-start.28 = (f32[2,128,256]{2,1,0:T(8,128)}, f32[2,128,256]{2,1,0:T(8,128)S(1)}, u32[]{:S(2)}) copy-start(f32[2,128,256]{2,1,0:T(8,128)S(1)} %get-tuple-element.10.wd_ref.refs_2_) | copy-start | bytes 786436
  53.4 14.3 %all-to-all-start.2 = ((bf16[16,96,128]{2,1,0:T(8,128)(2,1)}), bf16[16,96,128]{2,1,0:T(8,128)(2,1)S(1)}, u32[]{:S(2)}, u32[]{:S(2)}) async-start(bf16[16,96,128]{2,1,0:T(8,128)(2,1)} %bitcast.14), calls=%async_computation.2 | async-start | bytes 786432 | tf_op jit(solution)/shard_map/all_to_all | solution.py:304
  58.1 6.2 %copy-start.33 = (bf16[2,1024,256]{2,1,0:T(8,128)(2,1)S(1)}, bf16[2,1024,256]{2,1,0:T(8,128)(2,1)}, u32[]{:S(2)}) copy-start(bf16[2,1024,256]{2,1,0:T(8,128)(2,1)} %param.11) | copy-start | bytes 3145732
  60.1 60.4 %collective-permute-start.5 = (bf16[1024,256]{1,0:T(8,128)(2,1)}, bf16[1024,256]{1,0:T(8,128)(2,1)}, u32[]{:S(2)}, u32[]{:S(2)}) collective-permute-start(bf16[1024,256]{1,0:T(8,128)(2,1)} %broadcast_select_fusion.3), channel_id=1, source_target_pairs={{0,16},{16,0},{32,48},{48,32},{64,80},{80,64},{96,112},{112,96},{1... | collective-permute-start | bytes 1572872 | tf_op jit(solution)/shard_map/ppermute | solution.py:39
  65.2 55.2 %collective-permute-start.7 = (bf16[1024,256]{1,0:T(8,128)(2,1)}, bf16[1024,256]{1,0:T(8,128)(2,1)}, u32[]{:S(2)}, u32[]{:S(2)}) collective-permute-start(bf16[1024,256]{1,0:T(8,128)(2,1)} %broadcast_select_fusion.2), channel_id=1, source_target_pairs={{0,16},{16,0},{32,48},{48,32},{64,80},{80,64},{96,112},{112,96},{1... | collective-permute-start | bytes 1572872 | tf_op jit(solution)/shard_map/ppermute | solution.py:39
  69.9 34.8 %all-to-all-start.3 = ((bf16[16,96,128]{2,1,0:T(8,128)(2,1)}), bf16[16,96,128]{2,1,0:T(8,128)(2,1)S(1)}, u32[]{:S(2)}, u32[]{:S(2)}) async-start(bf16[16,96,128]{2,1,0:T(8,128)(2,1)} %broadcast_in_dim.7), calls=%async_computation.3 | async-start | bytes 786432 | tf_op jit(solution)/shard_map/all_to_all | solution.py:307
  74.2 0.7 copy-start.20
  74.9 1.0 copy-start.1
  75.9 1.0 copy-start.3
  77.0 1.0 copy-start.5
  78.0 0.9 copy-start.10
  79.0 0.9 copy-start.14
  79.9 0.9 copy-start.18
  103.8 0.8 copy-start.6
  104.6 1.0 copy-start.11
  105.6 0.9 copy-start.15
  106.5 0.9 copy-start.19
  107.5 0.9 copy-start.23
  108.4 0.9 copy-start.26
  109.4 0.9 copy-start.29
  119.4 1.1 copy-start.4
  119.4 1.3 copy-start.24
  119.4 1.5 copy-start.27
  119.4 1.5 %copy-start.30 = (f32[2,128,256]{2,1,0:T(8,128)S(1)}, f32[2,128,256]{2,1,0:T(8,128)}, u32[]{:S(2)}) copy-start(f32[2,128,256]{2,1,0:T(8,128)} %copy-done.28) | copy-start | bytes 786436
  121.0 23.3 %copy-start.7 = (bf16[1024,256]{1,0:T(8,128)(2,1)S(1)}, bf16[1024,256]{1,0:T(8,128)(2,1)}, u32[]{:S(2)}) copy-start(bf16[1024,256]{1,0:T(8,128)(2,1)} %copy-done.6) | copy-start | bytes 1572868
where the time goes:
time: 147 us; the launch traced here: 145 us
  Pallas kernels  69.9 us (48%)
  starting transfers between devices  26.7 us (18%)
  local copies, waits for them, and re-layouts  23.3 us (16%)
  waiting for transfers between devices  14.8 us (10%)
  other arithmetic  9.64 us (7%)
    pallas_call x2, Pallas kernels, mix(): pl.pallas_call(functools.partial(mix_kernel, first_group), out_shape=jax....  46.2 us
    pallas_call x2, Pallas kernels, step(): pl.pallas_call(step_kernel, out_shape=[jax.ShapeDtypeStruct(w.shape, f32)...  18.2 us
    unnamed x70, local copies, waits for them, and re-layouts  16.6 us
    all_to_all x2, starting transfers between devices, sum_over_seq(): arrived = lax.all_to_all(tiles, 'seq', 0, 0, tiled=True)  11.2 us
    all_to_all x2, starting transfers between devices, sum_over_seq(): lax.all_to_all(copies, 'seq', 0, 0, tiled=True).reshape(partial.shape)  8.22 us
    all_to_all x2, waiting for transfers between devices, sum_over_seq(): arrived = lax.all_to_all(tiles, 'seq', 0, 0, tiled=True)  7.8 us
    ppermute x8, starting transfers between devices, move(): lax.ppermute(block, 'seq', [(i, route(i)) for i in range(lax.axis_size('s...  7.25 us
    select_n x4, other arithmetic, body(): jnp.where(rank % 2 == 0, a, b)  6.29 us
  transfers between devices with their start and end apart: 12, of which 5 were waited for; matrix products, arithmetic and copies ran while one was open for 10% of the time, Pallas kernels for 32%

commit v1 on v0

v1 whole, which is shorter than its diff:
```python
import functools
import math

import jax
import jax.numpy as jnp
from jax import lax
from jax.experimental import pallas as pl
from jax.experimental.pallas import tpu as pltpu
from jax.sharding import PartitionSpec as P

HD = 128
FW = 256
NS_STEPS = 5
ROWS = 256

coeff_first = 3.4445
coeff_second = -4.775
coeff_third = 2.0315
frob_epsilon = 1e-07
rms_epsilon = 1e-06
column_epsilon = 1e-06

f32 = jnp.float32
bf16 = jnp.bfloat16
LEAST_SUM = 1e-25
MOST_SUM = 1e30
VMEM_LIMIT = 62 * 1024 * 1024
SMALL_LIMIT = 24 * 1024 * 1024
STEP_LIMIT = 24 * 1024 * 1024


def dot(a, b, over=((1,), (0,))):
    return lax.dot_general(a, b, (over, ((), ())), preferred_element_type=f32)


def sigmoid(x):
    return 0.5 * jnp.tanh(0.5 * x) + 0.5


def move(block, route):
    return lax.ppermute(block, "seq", [(i, route(i)) for i in range(lax.axis_size("seq"))])


def fetch(copies, sems, at=0):
    started = [pltpu.make_async_copy(a, b, sems.at[at + i]) for i, (a, b) in enumerate(copies)]
    for copy in started:
        copy.start()
    return started


def fetch(copies, sems, at=0):
    started = [pltpu.make_async_copy(a, b, sems.at[at + i]) for i, (a, b) in enumerate(copies)]
    for copy in started:
        copy.start()
    return started


def grads_kernel(k_ref, v_ref, r_ref, *refs):
    *w_refs, out_ref, grad_ref, hid_ref, og_ref = refs
    if len(w_refs) > 1:
        step_ref, *w_refs, kept_ref, limits_ref = w_refs
        for which in range(3):
            weight = w_refs[which][...]
            kept_ref[which] = weight
            limits_ref[which, :, :1] = jnp.sqrt(jnp.sum(weight * weight, axis=1, keepdims=True))
            for h in range(weight.shape[0]):
                limits_ref[which, h, 1:] = jnp.full((1, FW), step_ref[h], f32)
    else:
        w_refs = [w_refs[0].at[which] for which in range(3)]
    tokens, width = k_ref.shape
    for h in range(width // HD):
        lanes = slice(h * HD, (h + 1) * HD)
        low_gate, low_up, low_down = (w_ref[h].astype(bf16) for w_ref in w_refs)
        for c in range(tokens // ROWS):
            rows = slice(c * ROWS, (c + 1) * ROWS)
            keys = k_ref[rows, lanes]
            rate = jnp.broadcast_to(r_ref[h : h + 1, rows], (HD, ROWS)).T
            out_grad = (-rate * v_ref[rows, lanes].astype(f32)).astype(bf16)
            gate_pre = dot(keys, low_gate)
            up_pre = dot(keys, low_up)
            hidden_grad = dot(out_grad, low_down)
            sig = sigmoid(gate_pre)
            active = gate_pre * sig
            og_ref[rows] = out_grad
            hid_ref[rows] = (active * up_pre).astype(bf16)
            grad_ref[rows, FW:] = (hidden_grad * active).astype(bf16)
            grad_ref[rows, :FW] = (
                hidden_grad * up_pre * sig * (1.0 + gate_pre * (1.0 - sig))
            ).astype(bf16)
        both = dot(k_ref[:, lanes], grad_ref[...], ((0,), (0,)))
        down = dot(og_ref[...], hid_ref[...], ((0,), (0,)))
        for which, full in enumerate((both[:, :FW], both[:, FW:], down)):
            for half in range(2):
                out_ref[which, h, half] = full[:, half * HD : (half + 1) * HD].astype(bf16)


def local_grads(group, keys, values, rates, weights, step_sizes=None):
    _, tokens, width = keys.shape
    heads = width // HD
    extra = [] if step_sizes is None else [step_sizes]
    group_rows = pl.BlockSpec((None, tokens, width), lambda i: (group, 0, 0))
    whole = [pl.BlockSpec(w.shape, lambda i, n=w.ndim: (0,) * n) for w in weights]
    out_shape = [jax.ShapeDtypeStruct((3, heads, 2, HD, HD), bf16)]
    if extra:
        out_shape = [
            jax.ShapeDtypeStruct((3, heads, HD, FW), f32),
            jax.ShapeDtypeStruct((3, heads, 2, FW), f32),
        ] + out_shape
    return pl.pallas_call(
        grads_kernel,
        out_shape=out_shape,
        grid=(1,),
        in_specs=[group_rows] * 2
        + [pl.BlockSpec((None, heads, tokens), lambda i: (group, 0, 0))]
        + [pl.BlockSpec(memory_space=pltpu.SMEM)] * len(extra)
        + whole,
        out_specs=[pl.BlockSpec(o.shape, lambda i, n=len(o.shape): (0,) * n) for o in out_shape],
        scratch_shapes=[
            pltpu.VMEM((tokens, 2 * FW), bf16),
            pltpu.VMEM((tokens, FW), bf16),
            pltpu.VMEM((tokens, HD), bf16),
        ],
        compiler_params=pltpu.CompilerParams(vmem_limit_bytes=VMEM_LIMIT),
        cost_estimate=pl.CostEstimate(
            flops=12 * heads * tokens * HD * FW,
            bytes_accessed=4 * tokens * width,
            transcendentals=heads * tokens * FW,
        ),
        name="local_grads",
    )(keys, values, rates, *extra, *weights)


def split(x):
    high = x.astype(bf16)
    return high, (x - high.astype(f32)).astype(bf16)


def sweeps(x_ref, count):
    def sweep(_, carry):
        pieces, grams, polynomials = [], [], []
        for m in range(count):
            high, low = split(x_ref[m])
            pieces.append((high, low))
            stacked = jnp.concatenate([high, low], axis=0)
            g = dot(stacked, stacked, ((1,), (1,)))
            grams.append(g[:HD, :HD] + (g[HD:, :HD] + g[:HD, HD:]) + g[HD:, HD:])
        for m in range(count):
            row = jnp.concatenate(split(grams[m]), axis=1)
            squared = dot(row, jnp.concatenate([row, row], axis=0))
            polynomials.append(
                coeff_second * grams[m] + coeff_third * (squared[:, :HD] + squared[:, HD:])
            )
        for m in range(count):
            high, low = pieces[m]
            row = jnp.concatenate(split(polynomials[m]), axis=1)
            product = dot(row, jnp.concatenate([high, high], axis=0)) + dot(
                row, jnp.concatenate([low, low], axis=0)
            )
            x_ref[m] = coeff_first * x_ref[m] + product
        return carry

    lax.fori_loop(0, NS_STEPS, sweep, 0)


def step_kernel(s_ref, w_hbm, limits_hbm, out_hbm, x_ref, w_ref, limits_ref, out_ref, sems):
    heads = out_ref.shape[1]
    started = fetch([(w_hbm, w_ref), (limits_hbm, limits_ref)], sems)
    for which in range(3):
        for h in range(heads):
            grad = jnp.concatenate([s_ref[which, h, 0], s_ref[which, h, 1]], axis=1).astype(f32)
            frobenius = jnp.sqrt(jnp.sum(grad * grad, keepdims=True))
            x_ref[which * heads + h] = grad / (frobenius + frob_epsilon)
    sweeps(x_ref, 3 * heads)
    for copy in started:
        copy.wait()
    written = []
    for which in range(3):
        for h in range(heads):
            target = limits_ref[which, h, :1]
            stepped = w_ref[which, h] - limits_ref[which, h, 1:] * x_ref[which * heads + h]
            length = jnp.sqrt(jnp.sum(stepped * stepped, axis=0, keepdims=True))
            out_ref[which, h] = stepped * (target / (length + column_epsilon))
        copy = pltpu.make_async_copy(out_ref.at[which], out_hbm.at[which], sems.at[2 + which])
        copy.start()
        written.append(copy)
    for copy in written:
        copy.wait()


def step(summed, weights, limits):
    heads = weights.shape[1]
    everywhere = pl.BlockSpec(memory_space=pl.ANY)
    return pl.pallas_call(
        step_kernel,
        out_shape=jax.ShapeDtypeStruct(weights.shape, f32),
        in_specs=[pl.BlockSpec(memory_space=pltpu.VMEM), everywhere, everywhere],
        out_specs=everywhere,
        scratch_shapes=[
            pltpu.VMEM((3 * heads, HD, FW), f32),
            pltpu.VMEM(weights.shape, f32),
            pltpu.VMEM(limits.shape, f32),
            pltpu.VMEM(weights.shape, f32),
            pltpu.SemaphoreType.DMA((5,)),
        ],
        compiler_params=pltpu.CompilerParams(vmem_limit_bytes=STEP_LIMIT),
        cost_estimate=pl.CostEstimate(
            flops=3 * heads * NS_STEPS * 40 * HD * HD * FW,
            bytes_accessed=3 * heads * 10 * HD * FW,
            transcendentals=0,
        ),
        name="weight_step",
    )(summed, weights, limits)


def mix_kernel(group, rank_ref, *refs):
    (
        q_hbm, k_hbm, v_hbm, ks_hbm, vs_hbm, kf_hbm, vf_hbm, kb_hbm, vb_hbm, w_hbm, gain_hbm,
        out_hbm, q_ref, ko_ref, vo_ref, kf_ref, vf_ref, kn_ref, vn_ref, w_ref, gain_ref,
        normed_ref, out_ref, sems,
    ) = refs
    tokens, width = q_ref.shape
    heads = width // HD
    scale = 1.0 / math.sqrt(HD)
    power = scale * math.log2(math.e)
    blocks = tokens // ROWS
    odd = rank_ref[0] % 2 == 1
    started = fetch(
        [
            (w_hbm, w_ref),
            (gain_hbm, gain_ref),
            (q_hbm.at[group], q_ref),
            (k_hbm.at[group], ko_ref),
            (v_hbm.at[group], vo_ref),
            (kf_hbm, kf_ref),
            (vf_hbm, vf_ref),
        ],
        sems,
    )
    beside = [(ks_hbm.at[group], kn_ref), (vs_hbm.at[group], vn_ref)]
    behind = [(kb_hbm, kn_ref), (vb_hbm, vn_ref)]

    @pl.when(odd)
    def _():
        fetch(beside, sems, 7)

    @pl.when(jnp.logical_not(odd))
    def _():
        fetch(behind, sems, 7)

    started += [pltpu.make_async_copy(a, b, sems.at[7 + i]) for i, (a, b) in enumerate(behind)]
    for copy in started[:3]:
        copy.wait()
    all_lanes = [slice(h * HD, (h + 1) * HD) for h in range(heads)]
    all_rows = [slice(b * ROWS, (b + 1) * ROWS) for b in range(blocks)]
    for h, lanes in enumerate(all_lanes):
        low_gate, low_up, low_down = (w_ref[which, h].astype(bf16) for which in range(3))
        for rows in all_rows:
            q = q_ref[rows, lanes]
            gate_pre = dot(q, low_gate)
            hidden = (gate_pre * sigmoid(gate_pre) * dot(q, low_up)).astype(bf16)
            applied = dot(hidden, low_down, ((1,), (1,)))
            mean = jnp.mean(applied * applied, axis=1, keepdims=True)
            normed_ref[rows, lanes] = applied * lax.rsqrt(mean + rms_epsilon) * gain_ref[:, lanes]
    for copy in started[3:]:
        copy.wait()

    near_valid = rank_ref[0] >= 1 if group == 0 else True
    far_valid = rank_ref[0] >= 2 if group == 0 else True

    def beside_ones(v, valid=True):
        wide = jnp.concatenate([v, jnp.ones((v.shape[0], HD), bf16)], axis=1)
        return wide if valid is True else wide * jnp.where(valid, 1.0, 0.0).astype(bf16)

    causal = lax.broadcasted_iota(jnp.int32, (ROWS, ROWS), 0) >= lax.broadcasted_iota(
        jnp.int32, (ROWS, ROWS), 1
    )

    def raised(q, keys):
        return jnp.exp2(dot(q, keys, ((1,), (1,))) * power).astype(bf16)

    wrong = jnp.zeros((ROWS, HD), f32)
    for lanes in all_lanes:
        for b, rows in enumerate(all_rows):
            q = q_ref[rows, lanes]
            own = dot(q, ko_ref[rows, lanes], ((1,), (1,)))
            far = dot(q, kf_ref[rows, lanes], ((1,), (1,)))
            edge = jnp.exp2(jnp.where(causal, own, far) * power)
            total = dot(
                jnp.where(causal, edge, 0.0).astype(bf16), beside_ones(vo_ref[rows, lanes])
            )
            total += dot(
                jnp.where(causal, 0.0, edge).astype(bf16),
                beside_ones(vf_ref[rows, lanes], far_valid),
            )
            total += dot(raised(q, kn_ref[:, lanes]), beside_ones(vn_ref[:, lanes], near_valid))
            if b > 0:
                past = slice(0, b * ROWS)
                total += dot(raised(q, ko_ref[past, lanes]), beside_ones(vo_ref[past, lanes]))
            if b < blocks - 1:
                rest = slice((b + 1) * ROWS, tokens)
                total += dot(
                    raised(q, kf_ref[rest, lanes]), beside_ones(vf_ref[rest, lanes], far_valid)
                )
            sums = total[:, HD:]
            out_ref[rows, lanes] = (normed_ref[rows, lanes] + total[:, :HD] / sums).astype(bf16)
            fine = (sums > LEAST_SUM) & (sums < MOST_SUM)
            wrong = jnp.maximum(wrong, jnp.where(fine, 0.0, 1.0))

    @pl.when(jnp.max(wrong) > 0.0)
    def _():
        def one_block(b, carry):
            rows = pl.ds(pl.multiple_of(b * ROWS, ROWS), ROWS)
            place = b * ROWS + lax.broadcasted_iota(jnp.int32, (ROWS, tokens), 0)
            column = lax.broadcasted_iota(jnp.int32, (ROWS, tokens), 1)
            limit = jnp.where(far_valid, tokens, -1)
            least = jnp.where(near_valid, 0, tokens)
            lowest = jnp.float32(-jnp.inf)
            for lanes in all_lanes:
                q = q_ref[rows, lanes]
                far = dot(q, kf_ref[:, lanes], ((1,), (1,))) * scale
                far = jnp.where((column > place) & (column < limit), far, lowest)
                near = dot(q, kn_ref[:, lanes], ((1,), (1,))) * scale
                near = jnp.where(column >= least, near, lowest)
                own = dot(q, ko_ref[:, lanes], ((1,), (1,))) * scale
                own = jnp.where(column <= place, own, lowest)
                parts = ((far, vf_ref), (near, vn_ref), (own, vo_ref))
                most = jnp.max(own, axis=1, keepdims=True)
                for scores, _ in parts[:2]:
                    most = jnp.maximum(most, jnp.max(scores, axis=1, keepdims=True))
                total = jnp.zeros((ROWS, HD), f32)
                sums = jnp.zeros((ROWS, 1), f32)
                for scores, v_ref in parts:
                    e = jnp.exp(scores - most)
                    sums += jnp.sum(e, axis=1, keepdims=True)
                    total += dot(e.astype(bf16), v_ref[:, lanes])
                out_ref[rows, lanes] = (normed_ref[rows, lanes] + total / sums).astype(bf16)
            return carry

        lax.fori_loop(0, blocks, one_block, 0)

    done = pltpu.make_async_copy(out_ref, out_hbm.at[group], sems.at[9])
    done.start()
    done.wait()


def mix(group, so_far, rank, queries, keys, values, early, context, weights, gain):
    groups, tokens, width = queries.shape
    heads = width // HD
    earlier = [] if so_far is None else [so_far]
    kernel = functools.partial(mix_kernel, group)
    if earlier:
        kernel = functools.partial(after_earlier, kernel)
    everywhere = pl.BlockSpec(memory_space=pl.ANY)
    block = pltpu.VMEM((tokens, width), bf16)
    return pl.pallas_call(
        kernel,
        out_shape=jax.ShapeDtypeStruct(queries.shape, bf16),
        in_specs=[everywhere] * len(earlier)
        + [pl.BlockSpec(memory_space=pltpu.SMEM)]
        + [everywhere] * 11,
        out_specs=everywhere,
        input_output_aliases={0: 0} if earlier else {},
        scratch_shapes=[block] * 7
        + [
            pltpu.VMEM(weights.shape, f32),
            pltpu.VMEM(gain.shape, f32),
            pltpu.VMEM((tokens, width), f32),
            block,
            pltpu.SemaphoreType.DMA((10,)),
        ],
        compiler_params=pltpu.CompilerParams(vmem_limit_bytes=VMEM_LIMIT),
        cost_estimate=pl.CostEstimate(
            flops=heads * tokens * 2 * tokens * 8 * HD,
            bytes_accessed=16 * tokens * width,
            transcendentals=heads * tokens * 2 * tokens,
        ),
        name="mix",
    )(*earlier, rank, queries, keys, values, *early, *context, weights, gain)


def after_earlier(kernel, _, *refs):
    kernel(*refs)


def add_kernel(x_ref, out_ref):
    total = jnp.sum(x_ref[...].astype(f32), axis=0).astype(bf16)
    for i in range(out_ref.shape[0]):
        out_ref[i] = total


def after(x, event):
    return lax.optimization_barrier((x, event))[0]


def exchange(tiles):
    return lax.all_to_all(tiles, "seq", 0, 0, tiled=True)


def add_parts(arrived):
    vmem = pl.BlockSpec(memory_space=pltpu.VMEM)
    return pl.pallas_call(
        add_kernel,
        out_shape=jax.ShapeDtypeStruct(arrived.shape, bf16),
        in_specs=[vmem],
        out_specs=vmem,
        compiler_params=pltpu.CompilerParams(vmem_limit_bytes=SMALL_LIMIT),
        name="add_parts",
    )(arrived)


def body(
    query_vectors,
    key_vectors,
    value_vectors,
    token_rates,
    gate_weight,
    up_weight,
    down_weight,
    step_sizes,
    norm_gain,
):
    rank = lax.axis_index("seq")
    size = lax.axis_size("seq")
    gain = norm_gain.reshape(1, -1)
    ranks = rank.astype(jnp.int32).reshape(1)

    def block_of(tensor, group):
        own = tensor[group]
        if group > 0:
            own = jnp.where(rank >= size - 2, tensor[group - 1], own)
        return own

    def send_far(block):
        return move(block, lambda i: (i + 2) % size)

    def swap(block):
        return move(block, lambda i: i ^ 1)

    def mix_group(group, so_far, early, context, weights):
        own = (query_vectors, key_vectors, value_vectors)
        return mix(group, so_far, ranks, *own, early, context, weights, gain)

    together = lax.optimization_barrier
    first = (gate_weight, up_weight, down_weight)
    blocks = [[block_of(t, g) for t in (key_vectors, value_vectors)] for g in range(2)]
    far_keys = send_far(blocks[0][0])
    weights, limits, partial = local_grads(
        0, key_vectors, value_vectors, token_rates, first, step_sizes
    )
    far_values = send_far(after(blocks[0][1], (far_keys, partial)))
    added = add_parts(exchange(partial.reshape(size, -1, HD)))
    summed = exchange(added)
    early = [swap(key_vectors), swap(value_vectors)]
    context = (far_keys, far_values, swap(far_keys), swap(far_values))
    far_keys = send_far(after(blocks[1][0], (far_values, summed)))
    later = step(summed.reshape(partial.shape), weights, limits)
    (partial,) = local_grads(1, key_vectors, value_vectors, token_rates, (later,))
    far_values = send_far(after(blocks[1][1], (far_keys, partial)))
    arrived = exchange(partial.reshape(size, -1, HD))
    mixed = mix_group(0, None, early, context, weights)
    arrived, mixed, far_keys, far_values = together((arrived, mixed, far_keys, far_values))
    summed = exchange(add_parts(arrived))
    context = (far_keys, far_values, swap(far_keys), swap(far_values))
    mixed = mix_group(1, mixed, early, context, later)
    summed, mixed = together((summed, mixed))
    last = step(summed.reshape(partial.shape), later, limits)
    return mixed, last


def solution(mesh):
    return jax.shard_map(
        body,
        mesh=mesh,
        in_specs=(
            P("batch", "seq", "head"),
            P("batch", "seq", "head"),
            P("batch", "seq", "head"),
            P("batch", "head", "seq"),
            P("head", None, None),
            P("head", None, None),
            P("head", None, None),
            P("head"),
            P("head"),
        ),
        out_specs=(P("batch", "seq", "head"), P("batch", "head", None, None)),
        check_vma=False,
    )
```

time: 147 us -> 119 us (0.81)
  local copies, waits for them, and re-layouts: 23.3 us -> 3.05 us
  other arithmetic: 9.64 us -> 2.58 us
  Pallas kernels: 69.9 us -> 64.7 us
  starting transfers between devices: 26.7 us -> 31.2 us
    unnamed x70 -> x10, local copies, waits for them, and re-layouts: 16.6 us -> 0.9 us
    pallas_call x6 -> x8, Pallas kernels: 69.9 us -> 64.7 us  [the longest x2 44.2 us: mix(): pl.pallas_call(kernel, out_shape=jax.ShapeDtypeStruct(queries.shape, bf16...]
    all_to_all x4, starting transfers between devices: 19.5 us -> 24.2 us  [exchange(): return lax.all_to_all(tiles, 'seq', 0, 0, tiled=True)]
    select_n x4 -> x2, other arithmetic: 6.29 us -> 2.58 us  [block_of(): own = jnp.where(rank >= size - 2, tensor[group - 1], own)]
    broadcast_in_dim x2 -> x0, local copies, waits for them, and re-layouts: 3.07 us -> none  [sum_over_seq(): copies = jnp.broadcast_to(part, tiles.shape)]
    all_to_all x4, waiting for transfers between devices: 8.91 us -> 11.2 us  [exchange(): return lax.all_to_all(tiles, 'seq', 0, 0, tiled=True)]
    another operation x2 -> x0, other arithmetic: 2.03 us -> none  [body(): return (jnp.stack(mixed), jnp.stack(weights))]
    squeeze x4 -> x2, local copies, waits for them, and re-layouts: 3.66 us -> 2.15 us  [block_of(): own = tensor[group]]
  transfers between devices with their start and end apart: 12 -> 14, of which waited for: 5 -> 4; matrix products, arithmetic and copies ran while one was open for 10% -> 3% of each run, Pallas kernels for 32% -> 50%
where the time goes in v1:
time: 119 us; the launch traced here: 118 us
  Pallas kernels  64.7 us (54%)
  starting transfers between devices  31.2 us (26%)
  waiting for transfers between devices  15.8 us (13%)
  local copies, waits for them, and re-layouts  3.05 us (3%)
  other arithmetic  2.58 us (2%)
    pallas_call x2, Pallas kernels, mix(): pl.pallas_call(kernel, out_shape=jax.ShapeDtypeStruct(queries.shape, bf16...  44.2 us
    all_to_all x4, starting transfers between devices, exchange(): return lax.all_to_all(tiles, 'seq', 0, 0, tiled=True)  24.2 us
    all_to_all x4, waiting for transfers between devices, exchange(): return lax.all_to_all(tiles, 'seq', 0, 0, tiled=True)  11.2 us
    pallas_call x2, Pallas kernels, step(): pl.pallas_call(step_kernel, out_shape=jax.ShapeDtypeStruct(weights.shape,...  10.3 us
    pallas_call x2, Pallas kernels, local_grads(): pl.pallas_call(grads_kernel, out_shape=out_shape, grid=(1,), in_specs=[gr...  8.56 us
    ppermute x10, starting transfers between devices, move(): lax.ppermute(block, 'seq', [(i, route(i)) for i in range(lax.axis_size('s...  7.02 us
    ppermute x10, waiting for transfers between devices, move(): lax.ppermute(block, 'seq', [(i, route(i)) for i in range(lax.axis_size('s...  4.58 us
    select_n x2, other arithmetic, block_of(): own = jnp.where(rank >= size - 2, tensor[group - 1], own)  2.58 us
  transfers between devices with their start and end apart: 14, of which 4 were waited for; matrix products, arithmetic and copies ran while one was open for 3% of the time, Pallas kernels for 50%

profile of v1, /device:TPU:1, one launch (start us, length us, event | category | flops | bytes accessed | tf_op | source)
XLA Modules:
  0.0 118.3 jit_solution(17530326829296538997)
XLA Ops:
  0.6 1.1 slice_bitcast_fusion.1
  1.7 2.2 %collective-permute-start.2 = (bf16[1024,256]{1,0:T(8,128)(2,1)S(1)}, bf16[1024,256]{1,0:T(8,128)(2,1)}, u32[]{:S(2)}, u32[]{:S(2)}) collective-permute-start(bf16[1024,256]{1,0:T(8,128)(2,1)S(1)} %slice_bitcast_fusion.1), channel_id=1, source_target_pairs={{0,32},{16,48},{32,64},{48,80},{64,96},{80,112},{96,128},{112,144}... | collective-permute-start | bytes 1572872 | tf_op jit(solution)/shard_map/ppermute | solution.py:41
  3.9 4.4 %local_grads.2 = (f32[3,2,128,256]{3,2,1,0:T(8,128)}, f32[3,2,2,256]{3,2,1,0:T(2,128)}, bf16[3,2,2,128,128]{4,3,2,1,0:T(8,128)(2,1)}) custom-call(bf16[2,1024,256]{2,1,0:T(8,128)(2,1)} %refs_2_.5, bf16[2,1024,256]{2,1,0:T(8,128)(2,1)} %refs_3_.3, f32[2,2,1024]{2,1,0:T(2,128)} %r_ref.3, f32[2]{0:T(128)} %refs_0_.2, f32[2,128,256]{2,1,0:T(8,128)} %refs_1_.3, ...), custom_call_target="tpu_custom_call" | custom-call | flops 805306368 | bytes 1048576 | tf_op jit(solution)/shard_map/local_grads/pallas_call | solution.py:109
  8.3 6.5 %all-to-all-start = ((bf16[16,96,128]{2,1,0:T(8,128)(2,1)}), bf16[16,96,128]{2,1,0:T(8,128)(2,1)S(1)}, u32[]{:S(2)}, u32[]{:S(2)}) async-start(bf16[16,96,128]{2,1,0:T(8,128)(2,1)} %bitcast.21), calls=%async_computation | async-start | bytes 786432 | tf_op jit(solution)/shard_map/all_to_all | solution.py:396
  14.8 1.1 slice_bitcast_fusion
  15.9 0.1 collective-permute-done.2.refs_5_
  16.0 1.3 %collective-permute-start.3 = (bf16[1024,256]{1,0:T(8,128)(2,1)S(1)}, bf16[1024,256]{1,0:T(8,128)(2,1)}, u32[]{:S(2)}, u32[]{:S(2)}) collective-permute-start(bf16[1024,256]{1,0:T(8,128)(2,1)S(1)} %slice_bitcast_fusion), channel_id=1, source_target_pairs={{0,32},{16,48},{32,64},{48,80},{64,96},{80,112},{96,128},{112,144}... | collective-permute-start | bytes 1572872 | tf_op jit(solution)/shard_map/ppermute | solution.py:41
  17.4 1.9 %collective-permute-start = (bf16[2,1024,256]{2,1,0:T(8,128)(2,1)}, bf16[2,1024,256]{2,1,0:T(8,128)(2,1)}, u32[]{:S(2)}, u32[]{:S(2)}) collective-permute-start(bf16[2,1024,256]{2,1,0:T(8,128)(2,1)} %refs_2_.5), channel_id=1, source_target_pairs={{0,16},{16,0},{32,48},{48,32},{64,80},{80,64},{96,112},{112,96},{1... | collective-permute-start | bytes 3145736 | tf_op jit(solution)/shard_map/ppermute | solution.py:41
  19.3 0.0 collective-permute-start.1
  19.3 3.9 %all-to-all-done.x_ref = bf16[16,96,128]{2,1,0:T(8,128)(2,1)S(1)} async-done(((bf16[16,96,128]{2,1,0:T(8,128)(2,1)}), bf16[16,96,128]{2,1,0:T(8,128)(2,1)S(1)}, u32[]{:S(2)}, u32[]{:S(2)}) %all-to-all-start) | async-done | bytes 393248 | tf_op jit(solution)/shard_map/all_to_all | solution.py:396
  23.2 0.8 add_parts.2
  24.0 5.0 %all-to-all-start.1 = ((bf16[16,96,128]{2,1,0:T(8,128)(2,1)}), bf16[16,96,128]{2,1,0:T(8,128)(2,1)S(1)}, u32[]{:S(2)}, u32[]{:S(2)}) async-start(bf16[16,96,128]{2,1,0:T(8,128)(2,1)} %add_parts.2), calls=%async_computation.1 | async-start | bytes 786432 | tf_op jit(solution)/shard_map/all_to_all | solution.py:396
  29.0 1.3 %bitcast_select_fusion.1 = bf16[1024,256]{1,0:T(8,128)(2,1)S(1)} fusion(bf16[2,1024,256]{2,1,0:T(8,128)(2,1)} %refs_2_.5, pred[]{:T(512)S(6)} %ge.4), kind=kLoop, calls=%fused_computation.1 | loop fusion | flops 262144 | bytes 1572865 | tf_op jit(solution)/shard_map/jit(_where)/select_n | solution.py:430
  30.2 0.0 copy-start.2
  30.3 0.0 copy-start.3
  30.3 1.3 %bitcast_select_fusion = bf16[1024,256]{1,0:T(8,128)(2,1)S(1)} fusion(bf16[2,1024,256]{2,1,0:T(8,128)(2,1)} %refs_3_.3, pred[]{:T(512)S(6)} %ge.4), kind=kLoop, calls=%fused_computation | loop fusion | flops 262144 | bytes 1572865 | tf_op jit(solution)/shard_map/jit(_where)/select_n | solution.py:430
  31.6 0.3 collective-permute-start.4
  31.9 7.2 %all-to-all-done.1 = bf16[16,96,128]{2,1,0:T(8,128)(2,1)S(1)} async-done(((bf16[16,96,128]{2,1,0:T(8,128)(2,1)}), bf16[16,96,128]{2,1,0:T(8,128)(2,1)S(1)}, u32[]{:S(2)}, u32[]{:S(2)}) %all-to-all-start.1) | async-done | bytes 393248 | tf_op jit(solution)/shard_map/all_to_all | solution.py:396
  39.2 0.0 collective-permute-done.3.refs_6_
  39.2 0.0 collective-permute-start.6
  39.2 0.7 collective-permute-start.5
  39.8 0.0 copy-done.2
  39.8 0.0 copy-done.3
  39.8 4.8 %weight_step.2.refs_0_.refs_10_.w_hbm = f32[3,2,128,256]{3,2,1,0:T(8,128)S(1)} custom-call(bf16[3,2,2,128,128]{4,3,2,1,0:T(8,128)(2,1)S(1)} %bitcast.18, f32[3,2,128,256]{3,2,1,0:T(8,128)S(1)} %copy-done.2, f32[3,2,2,256]{3,2,1,0:T(2,128)S(1)} %copy-done.3), custom_call_target="tpu_custom_call" | custom-call | flops 5033164800 | bytes 1966080 | tf_op jit(solution)/shard_map/weight_step/pallas_call | solution.py:193
  44.7 0.0 copy-start
  44.7 0.9 copy-done
  45.6 4.2 %local_grads.3 = bf16[3,2,2,128,128]{4,3,2,1,0:T(8,128)(2,1)} custom-call(bf16[2,1024,256]{2,1,0:T(8,128)(2,1)} %refs_2_.5, bf16[2,1024,256]{2,1,0:T(8,128)(2,1)} %refs_3_.3, f32[2,2,1024]{2,1,0:T(2,128)} %r_ref.3, f32[3,2,128,256]{3,2,1,0:T(8,128)} %copy-done), custom_call_target="tpu_custom_call" | custom-call | flops 805306368 | bytes 1048576 | tf_op jit(solution)/shard_map/local_grads/pallas_call | solution.py:109
  49.8 4.4 %collective-permute-done.6.refs_6_ = bf16[1024,256]{1,0:T(8,128)(2,1)} collective-permute-done((bf16[1024,256]{1,0:T(8,128)(2,1)S(1)}, bf16[1024,256]{1,0:T(8,128)(2,1)}, u32[]{:S(2)}, u32[]{:S(2)}) %collective-permute-start.6) | collective-permute-done | bytes 524320 | tf_op jit(solution)/shard_map/ppermute | solution.py:41
  54.2 0.0 collective-permute-start.7
  54.2 7.0 %all-to-all-start.2 = ((bf16[16,96,128]{2,1,0:T(8,128)(2,1)}), bf16[16,96,128]{2,1,0:T(8,128)(2,1)S(1)}, u32[]{:S(2)}, u32[]{:S(2)}) async-start(bf16[16,96,128]{2,1,0:T(8,128)(2,1)} %bitcast.20), calls=%async_computation.2 | async-start | bytes 786432 | tf_op jit(solution)/shard_map/all_to_all | solution.py:396
  61.1 0.0 collective-permute-done.4.refs_7_
  61.1 0.0 collective-permute-done.refs_3_.refs_4_
  61.2 0.0 collective-permute-done.1.refs_4_.refs_5_
  61.2 0.0 collective-permute-done.5.refs_8_
  61.2 22.2 %mix.2._ = bf16[2,1024,256]{2,1,0:T(8,128)(2,1)} custom-call(s32[1]{0:T(128)} %bitcast.3.rank_ref.refs_0_, bf16[2,1024,256]{2,1,0:T(8,128)(2,1)} %refs_1_.5, bf16[2,1024,256]{2,1,0:T(8,128)(2,1)} %refs_2_.5, bf16[2,1024,256]{2,1,0:T(8,128)(2,1)} %refs_3_.3, bf16[2,1024,256]{2,1,0:T(8,128)(2,1)} %collective-permute-done.refs_3_.refs_4_, ...), custom_call_target="tpu_custom_call" | custom-call | flops 4294967296 | bytes 4194304 | tf_op jit(solution)/shard_map/mix/pallas_call | solution.py:355
  83.4 0.0 all-to-all-done.2.x_ref
  83.4 0.0 collective-permute-done.7.refs_7_
  83.4 0.0 copy-start.4
  83.4 0.2 collective-permute-start.8
  83.6 0.4 collective-permute-start.9
  84.0 0.8 add_parts.3
  84.8 0.0 copy-done.4
  84.9 5.7 %all-to-all-start.3 = ((bf16[16,96,128]{2,1,0:T(8,128)(2,1)}), bf16[16,96,128]{2,1,0:T(8,128)(2,1)S(1)}, u32[]{:S(2)}, u32[]{:S(2)}) async-start(bf16[16,96,128]{2,1,0:T(8,128)(2,1)} %add_parts.3), calls=%async_computation.3 | async-start | bytes 786432 | tf_op jit(solution)/shard_map/all_to_all | solution.py:396
  90.6 0.0 collective-permute-done.8.refs_8_
  90.6 0.0 collective-permute-done.9.refs_9_
  90.6 22.0 %mix.3 = bf16[2,1024,256]{2,1,0:T(8,128)(2,1)} custom-call(bf16[2,1024,256]{2,1,0:T(8,128)(2,1)} %mix.2._, s32[1]{0:T(128)} %bitcast.3.rank_ref.refs_0_, bf16[2,1024,256]{2,1,0:T(8,128)(2,1)} %refs_1_.5, bf16[2,1024,256]{2,1,0:T(8,128)(2,1)} %refs_2_.5, bf16[2,1024,256]{2,1,0:T(8,128)(2,1)} %refs_3_.3, ...), custom_call_target="tpu_custom_call", output_to_operand_aliasing={{}: (0, {})} | custom-call | flops 4294967296 | bytes 4194304 | tf_op jit(solution)/shard_map/mix/pallas_call | solution.py:355
  112.6 0.0 all-to-all-done.3
  112.6 5.5 %weight_step.3 = f32[3,2,128,256]{3,2,1,0:T(8,128)} custom-call(bf16[3,2,2,128,128]{4,3,2,1,0:T(8,128)(2,1)S(1)} %bitcast.19, f32[3,2,128,256]{3,2,1,0:T(8,128)S(1)} %copy-done.1, f32[3,2,2,256]{3,2,1,0:T(2,128)S(1)} %copy-done.3), custom_call_target="tpu_custom_call" | custom-call | flops 5033164800 | bytes 1966080 | tf_op jit(solution)/shard_map/weight_step/pallas_call | solution.py:193
  (2 shorter events, 0.0 us)
Async XLA Ops:
  1.7 14.3 %collective-permute-start.2 = (bf16[1024,256]{1,0:T(8,128)(2,1)S(1)}, bf16[1024,256]{1,0:T(8,128)(2,1)}, u32[]{:S(2)}, u32[]{:S(2)}) collective-permute-start(bf16[1024,256]{1,0:T(8,128)(2,1)S(1)} %slice_bitcast_fusion.1), channel_id=1, source_target_pairs={{0,32},{16,48},{32,64},{48,80},{64,96},{80,112},{96,128},{112,144}... | collective-permute-start | bytes 1572872 | tf_op jit(solution)/shard_map/ppermute | solution.py:41
  8.3 14.9 %all-to-all-start = ((bf16[16,96,128]{2,1,0:T(8,128)(2,1)}), bf16[16,96,128]{2,1,0:T(8,128)(2,1)S(1)}, u32[]{:S(2)}, u32[]{:S(2)}) async-start(bf16[16,96,128]{2,1,0:T(8,128)(2,1)} %bitcast.21), calls=%async_computation | async-start | bytes 786432 | tf_op jit(solution)/shard_map/all_to_all | solution.py:396
  16.0 23.1 %collective-permute-start.3 = (bf16[1024,256]{1,0:T(8,128)(2,1)S(1)}, bf16[1024,256]{1,0:T(8,128)(2,1)}, u32[]{:S(2)}, u32[]{:S(2)}) collective-permute-start(bf16[1024,256]{1,0:T(8,128)(2,1)S(1)} %slice_bitcast_fusion), channel_id=1, source_target_pairs={{0,32},{16,48},{32,64},{48,80},{64,96},{80,112},{96,128},{112,144}... | collective-permute-start | bytes 1572872 | tf_op jit(solution)/shard_map/ppermute | solution.py:41
  17.4 43.8 %collective-permute-start = (bf16[2,1024,256]{2,1,0:T(8,128)(2,1)}, bf16[2,1024,256]{2,1,0:T(8,128)(2,1)}, u32[]{:S(2)}, u32[]{:S(2)}) collective-permute-start(bf16[2,1024,256]{2,1,0:T(8,128)(2,1)} %refs_2_.5), channel_id=1, source_target_pairs={{0,16},{16,0},{32,48},{48,32},{64,80},{80,64},{96,112},{112,96},{1... | collective-permute-start | bytes 3145736 | tf_op jit(solution)/shard_map/ppermute | solution.py:41
  19.3 41.9 %collective-permute-start.1 = (bf16[2,1024,256]{2,1,0:T(8,128)(2,1)}, bf16[2,1024,256]{2,1,0:T(8,128)(2,1)}, u32[]{:S(2)}, u32[]{:S(2)}) collective-permute-start(bf16[2,1024,256]{2,1,0:T(8,128)(2,1)} %refs_3_.3), channel_id=1, source_target_pairs={{0,16},{16,0},{32,48},{48,32},{64,80},{80,64},{96,112},{112,96},{1... | collective-permute-start | bytes 3145736 | tf_op jit(solution)/shard_map/ppermute | solution.py:41
  24.0 15.2 %all-to-all-start.1 = ((bf16[16,96,128]{2,1,0:T(8,128)(2,1)}), bf16[16,96,128]{2,1,0:T(8,128)(2,1)S(1)}, u32[]{:S(2)}, u32[]{:S(2)}) async-start(bf16[16,96,128]{2,1,0:T(8,128)(2,1)} %add_parts.2), calls=%async_computation.1 | async-start | bytes 786432 | tf_op jit(solution)/shard_map/all_to_all | solution.py:396
  30.2 9.6 %copy-start.2 = (f32[3,2,128,256]{3,2,1,0:T(8,128)S(1)}, f32[3,2,128,256]{3,2,1,0:T(8,128)}, u32[]{:S(2)}) copy-start(f32[3,2,128,256]{3,2,1,0:T(8,128)} %get-tuple-element.15.w_hbm.refs_9_) | copy-start | bytes 2359300
  30.3 9.6 %copy-start.3 = (f32[3,2,2,256]{3,2,1,0:T(2,128)S(1)}, f32[3,2,2,256]{3,2,1,0:T(2,128)}, u32[]{:S(2)}) copy-start(f32[3,2,2,256]{3,2,1,0:T(2,128)} %get-tuple-element.16.limits_hbm) | copy-start | bytes 36868
  31.6 29.5 %collective-permute-start.4 = (bf16[1024,256]{1,0:T(8,128)(2,1)}, bf16[1024,256]{1,0:T(8,128)(2,1)}, u32[]{:S(2)}, u32[]{:S(2)}) collective-permute-start(bf16[1024,256]{1,0:T(8,128)(2,1)} %collective-permute-done.2.refs_5_), channel_id=1, source_target_pairs={{0,16},{16,0},{32,48},{48,32},{64,80},{80,64},{96,112},{112,96},{1... | collective-permute-start | bytes 1572872 | tf_op jit(solution)/shard_map/ppermute | solution.py:41
  39.2 15.0 %collective-permute-start.6 = (bf16[1024,256]{1,0:T(8,128)(2,1)S(1)}, bf16[1024,256]{1,0:T(8,128)(2,1)}, u32[]{:S(2)}, u32[]{:S(2)}) collective-permute-start(bf16[1024,256]{1,0:T(8,128)(2,1)S(1)} %bitcast_select_fusion.1), channel_id=1, source_target_pairs={{0,32},{16,48},{32,64},{48,80},{64,96},{80,112},{96,128},{112,144}... | collective-permute-start | bytes 1572872 | tf_op jit(solution)/shard_map/ppermute | solution.py:41
  39.2 22.0 %collective-permute-start.5 = (bf16[1024,256]{1,0:T(8,128)(2,1)}, bf16[1024,256]{1,0:T(8,128)(2,1)}, u32[]{:S(2)}, u32[]{:S(2)}) collective-permute-start(bf16[1024,256]{1,0:T(8,128)(2,1)} %collective-permute-done.3.refs_6_), channel_id=1, source_target_pairs={{0,16},{16,0},{32,48},{48,32},{64,80},{80,64},{96,112},{112,96},{1... | collective-permute-start | bytes 1572872 | tf_op jit(solution)/shard_map/ppermute | solution.py:41
  44.7 0.9 copy-start
  54.2 29.2 %collective-permute-start.7 = (bf16[1024,256]{1,0:T(8,128)(2,1)S(1)}, bf16[1024,256]{1,0:T(8,128)(2,1)S(1)}, u32[]{:S(2)}, u32[]{:S(2)}) collective-permute-start(bf16[1024,256]{1,0:T(8,128)(2,1)S(1)} %bitcast_select_fusion), channel_id=1, source_target_pairs={{0,32},{16,48},{32,64},{48,80},{64,96},{80,112},{96,128},{112,144}... | collective-permute-start | bytes 1572872 | tf_op jit(solution)/shard_map/ppermute | solution.py:41
  54.2 29.2 %all-to-all-start.2 = ((bf16[16,96,128]{2,1,0:T(8,128)(2,1)}), bf16[16,96,128]{2,1,0:T(8,128)(2,1)S(1)}, u32[]{:S(2)}, u32[]{:S(2)}) async-start(bf16[16,96,128]{2,1,0:T(8,128)(2,1)} %bitcast.20), calls=%async_computation.2 | async-start | bytes 786432 | tf_op jit(solution)/shard_map/all_to_all | solution.py:396
  83.4 1.5 %copy-start.4 = (bf16[1024,256]{1,0:T(8,128)(2,1)}, bf16[1024,256]{1,0:T(8,128)(2,1)S(1)}, u32[]{:S(2)}) copy-start(bf16[1024,256]{1,0:T(8,128)(2,1)S(1)} %collective-permute-done.7.refs_7_) | copy-start | bytes 1572868
  83.4 7.2 %collective-permute-start.8 = (bf16[1024,256]{1,0:T(8,128)(2,1)}, bf16[1024,256]{1,0:T(8,128)(2,1)}, u32[]{:S(2)}, u32[]{:S(2)}) collective-permute-start(bf16[1024,256]{1,0:T(8,128)(2,1)} %collective-permute-done.6.refs_6_), channel_id=1, source_target_pairs={{0,16},{16,0},{32,48},{48,32},{64,80},{80,64},{96,112},{112,96},{1... | collective-permute-start | bytes 1572872 | tf_op jit(solution)/shard_map/ppermute | solution.py:41
  83.6 7.0 %collective-permute-start.9 = (bf16[1024,256]{1,0:T(8,128)(2,1)S(1)}, bf16[1024,256]{1,0:T(8,128)(2,1)}, u32[]{:S(2)}, u32[]{:S(2)}) collective-permute-start(bf16[1024,256]{1,0:T(8,128)(2,1)S(1)} %collective-permute-done.7.refs_7_), channel_id=1, source_target_pairs={{0,16},{16,0},{32,48},{48,32},{64,80},{80,64},{96,112},{112,96},{1... | collective-permute-start | bytes 1572872 | tf_op jit(solution)/shard_map/ppermute | solution.py:41
  84.9 27.8 %all-to-all-start.3 = ((bf16[16,96,128]{2,1,0:T(8,128)(2,1)}), bf16[16,96,128]{2,1,0:T(8,128)(2,1)S(1)}, u32[]{:S(2)}, u32[]{:S(2)}) async-start(bf16[16,96,128]{2,1,0:T(8,128)(2,1)} %add_parts.3), calls=%async_computation.3 | async-start | bytes 786432 | tf_op jit(solution)/shard_map/all_to_all | solution.py:396
  90.6 22.0 %copy-start.1 = (f32[3,2,128,256]{3,2,1,0:T(8,128)S(1)}, f32[3,2,128,256]{3,2,1,0:T(8,128)}, u32[]{:S(2)}) copy-start(f32[3,2,128,256]{3,2,1,0:T(8,128)} %copy-done) | copy-start | bytes 2359300
